TPU v7x, 256 devices: a whole 4x4x8 slice. The times are simulated.
256 devices in a mesh: row: 32 (over z, y), col: 8 (over x, core).
Axes of the slice: x: 4, y: 4, z: 8, core: 2. Of those that a mesh axis runs over, the one named last changes fastest.
Arguments:
- tokens: bfloat16 [4096, 5120], P('row', 'col'), may hold values from -6 to 6
- target: bfloat16 [4096, 5120], P('row', 'col'), may hold values from -6 to 6
- w_gate: bfloat16 [5120, 13824], P('col', 'row'), may hold values from -0.078125 to 0.078125
- w_up: bfloat16 [5120, 13824], P('col', 'row'), may hold values from -0.078125 to 0.078125
- w_down: bfloat16 [13824, 5120], P('row', 'col'), may hold values from -0.0546875 to 0.0546875
- factor_u: bfloat16 [5120, 256], P('col'), may hold values from -0.078125 to 0.078125
- factor_v: bfloat16 [256, 13824], P(None, 'row'), may hold values from -3 to 3
Outputs:
- mixed: bfloat16 [4096, 5120], P('row', 'col')
- fitness: float32 [64], replicated
- update: float32 [5120, 13824], P('col', 'row')
All inputs are finite; a program needn't handle non-finite values.
Results may differ from a plain program's by a relative error of at most 0.0049.
Values may be sent and summed in bfloat16 or wider, within the bound.
No kernel may reach another device: no remote copies, remote signals or barrier semaphores. Data moves between devices by JAX's collectives and lax.ppermute only.
A program may use at most 128 MiB of HBM per device.

v0:
```python
import math
import jax
import jax.numpy as jnp
from jax import lax
from jax.sharding import PartitionSpec as P

D = 5120
RANK = 4
SEQ = 64
sigma_scale = 0.5


def apply_factors(low_three, v_three):
    return jnp.einsum("psr,prf->psf", low_three, v_three, precision=lax.Precision.HIGHEST)


def body(tokens, target, w_gate, w_up, w_down, factor_u, factor_v):
    dev_rows, dev_feat = tokens.shape
    members = factor_u.shape[1] // RANK
    units = w_up.shape[1]
    every = lax.all_gather(tokens, "row", axis=0, tiled=True)
    total_rows = every.shape[0]
    gate_part = jnp.dot(every, w_gate, preferred_element_type=jnp.float32)
    up_part = jnp.dot(every, w_up, preferred_element_type=jnp.float32)
    grouped = every.reshape(members, SEQ, dev_feat)
    u_three = factor_u.reshape(dev_feat, members, RANK)
    v_three = factor_v.reshape(members, RANK, units).astype(jnp.float32)
    low_part = jnp.einsum("psd,dpr->psr", grouped, u_three, preferred_element_type=jnp.float32)
    up_part = up_part + sigma_scale * apply_factors(low_part, v_three).reshape(total_rows, units)
    gate, up = (
        lax.psum_scatter(gate_part, "col", scatter_dimension=0, tiled=True),
        lax.psum_scatter(up_part, "col", scatter_dimension=0, tiled=True),
    )
    hidden = (jax.nn.silu(gate) * up).astype(jnp.bfloat16)
    hidden_all = lax.all_gather(hidden, "col", axis=0, tiled=True)
    out = lax.psum_scatter(
        jnp.dot(hidden_all, w_down, preferred_element_type=jnp.float32),
        "row",
        scatter_dimension=0,
        tiled=True,
    )
    mixed = out.astype(jnp.bfloat16)
    local_members = dev_rows // SEQ
    prod = (out * target.astype(jnp.float32)).reshape(local_members, SEQ * dev_feat)
    score = jnp.sum(prod, axis=1) / math.sqrt(SEQ * D)
    placed = lax.dynamic_update_slice(
        jnp.zeros((members,), jnp.float32), score, (lax.axis_index("row") * local_members,)
    )
    fitness = lax.psum(placed, ("row", "col"))
    weights = jnp.repeat(fitness, RANK)
    update = jnp.dot(
        factor_u.astype(jnp.float32) * weights[None, :],
        factor_v.astype(jnp.float32),
        precision=lax.Precision.HIGHEST,
        preferred_element_type=jnp.float32,
    ) * math.sqrt(D / members)
    return (mixed, fitness, update)


def solution(mesh):
    return jax.shard_map(
        body,
        mesh=mesh,
        in_specs=(
            P("row", "col"),
            P("row", "col"),
            P("col", "row"),
            P("col", "row"),
            P("row", "col"),
            P("col", None),
            P(None, "row"),
        ),
        out_specs=(P("row", "col"), P(), P("col", "row")),
        check_vma=False,
    )
```

profile of v0, /device:TPU:1, one launch (start us, length us, event | category | flops | bytes accessed | tf_op | source)
XLA Modules:
  0.0 587.6 jit_solution(11700659747309950121)
XLA Ops:
  7.2 0.0 copy-start
  7.2 0.0 all-gather.3.cloned.1.call-start
  7.2 0.7 all-gather.3.cloned.1.call-update
  7.9 0.0 reduce-scatter.6.cloned.1.call-start
  8.0 1.2 copy.12
  9.1 0.1 reshape.22
  9.2 1.1 copy.13
  10.3 0.1 reshape.23
  10.4 86.9 %all-gather.3.cloned.1.call-done = bf16[4096,640]{1,0:T(8,128)(2,1)} async-done(((bf16[128,640]{1,0:T(8,128)(2,1)}), bf16[4096,640]{1,0:T(8,128)(2,1)}) %all-gather.3.cloned.1.call-update) | async-done | bytes 5242896 | tf_op jit(solution)/shard_map/all_gather | solution.py:21
  97.3 4.2 fusion.4
  101.5 5.8 broadcast_multiply_fusion
  107.3 0.0 copy-start.3
  107.3 8.6 %copy.14 = f32[4096,432]{0,1:T(8,128)} copy(f32[4096,432]{1,0:T(8,128)} %bitcast.15) | data formatting | bytes 14155776 | tf_op jit(solution)/shard_map/mul | solution.py:29
  115.9 0.0 copy-done.3
  115.9 9.4 %convolution_add_fusion = f32[4096,432]{0,1:T(8,128)} fusion(f32[4096,432]{0,1:T(8,128)} %copy.14, bf16[4096,640]{1,0:T(8,128)(2,1)} %all-gather.3.cloned.1.call-done, bf16[640,432]{0,1:T(8,128)(2,1)S(1)} %copy-done.3), kind=kOutput, calls=%fused_computation | convolution fusion | flops 2266693632 | bytes 19951616 | tf_op jit(solution)/shard_map/dot_general | solution.py:24
  125.3 0.0 copy-start.6
  125.3 0.0 reduce-scatter.6.cloned.1.call-update
  125.4 0.0 reduce-scatter.4.cloned.1.call-start
  125.4 1.0 copy-done.6
  126.4 8.3 %fusion.3 = f32[4096,432]{0,1:T(8,128)} fusion(bf16[4096,640]{1,0:T(8,128)(2,1)} %all-gather.3.cloned.1.call-done, bf16[640,432]{0,1:T(8,128)(2,1)S(1)} %copy-done.6), kind=kOutput, calls=%fused_computation.9 | convolution fusion | flops 2264924160 | bytes 12873728 | tf_op jit(solution)/shard_map/dot_general | solution.py:23
  134.7 0.0 reduce-scatter.4.cloned.1.call-update
  134.7 0.0 all-gather.5.cloned.1.call-start
  134.8 38.4 %reduce-scatter.6.cloned.1.call-done = f32[512,432]{0,1:T(8,128)} async-done(((f32[4096,432]{0,1:T(8,128)}), f32[512,432]{0,1:T(8,128)}) %reduce-scatter.6.cloned.1.call-update) | async-done | bytes 884752 | tf_op jit(solution)/shard_map/reduce_scatter | solution.py:32
  173.2 51.0 %reduce-scatter.4.cloned.1.call-done = f32[512,432]{0,1:T(8,128)} async-done(((f32[4096,432]{0,1:T(8,128)}), f32[512,432]{0,1:T(8,128)}) %reduce-scatter.4.cloned.1.call-update) | async-done | bytes 884752 | tf_op jit(solution)/shard_map/reduce_scatter | solution.py:31
  224.2 2.5 multiply_convert_fusion
  226.6 0.0 all-gather.5.cloned.1.call-update
  226.6 0.0 reduce-scatter.8.cloned.1.call-start
  226.7 32.6 %all-gather.5.cloned.1.call-done = bf16[4096,432]{0,1:T(8,128)(2,1)} async-done(((bf16[512,432]{0,1:T(8,128)(2,1)}), bf16[4096,432]{0,1:T(8,128)(2,1)}) %all-gather.5.cloned.1.call-update) | async-done | bytes 3538960 | tf_op jit(solution)/shard_map/all_gather | solution.py:35
  259.3 0.0 copy-done
  259.3 9.5 %fusion.5 = f32[4096,640]{1,0:T(8,128)} fusion(bf16[4096,432]{0,1:T(8,128)(2,1)} %all-gather.5.cloned.1.call-done, bf16[432,640]{1,0:T(8,128)(2,1)S(1)} %copy-done), kind=kOutput, calls=%fused_computation.11 | convolution fusion | flops 2264924160 | bytes 14577664 | tf_op jit(solution)/shard_map/dot_general | solution.py:37
  268.8 0.0 copy-start.4
  268.8 0.0 copy-start.1
  268.8 0.0 copy-start.2
  268.8 0.0 reduce-scatter.8.cloned.1.call-update
  268.8 229.8 %reduce-scatter.8.cloned.1.call-done = f32[128,640]{1,0:T(8,128)} async-done(((f32[4096,640]{1,0:T(8,128)}), f32[128,640]{1,0:T(8,128)}) %reduce-scatter.8.cloned.1.call-update) | async-done | bytes 327696 | tf_op jit(solution)/shard_map/reduce_scatter | solution.py:36
  498.6 0.0 copy-done.4
  498.6 1.8 multiply_reduce_fusion
  500.4 0.1 reduce_sum.14
  500.5 0.1 reduce_sum.18
  500.6 0.1 multiply_dynamic-update-slice_fusion
  500.7 78.4 %psum.7 = f32[64]{0:T(128)S(1)} all-reduce(f32[64]{0:T(128)S(1)} %multiply_dynamic-update-slice_fusion), channel_id=1, replica_groups=mesh['row'=32,'col'=8] {'row','col'}, use_global_device_ids=true, to_apply=%region_5.6 | all-reduce | flops 64 | bytes 512 | tf_op jit(solution)/shard_map/psum | solution.py:49
  579.1 0.0 copy-start.5
  579.1 0.1 broadcast_in_dim.7
  579.2 0.1 mul.45
  579.3 0.0 copy-done.1
  579.3 0.0 copy-done.2
  579.3 1.8 convolution_multiply_fusion
  581.1 0.0 copy-done.5
  (1 shorter events, 0.0 us)
Async XLA Ops:
  7.2 252.2 %copy-start = (bf16[432,640]{1,0:T(8,128)(2,1)S(1)}, bf16[432,640]{1,0:T(8,128)(2,1)}, u32[]{:S(2)}) copy-start(bf16[432,640]{1,0:T(8,128)(2,1)} %param.11) | copy-start | bytes 1658884
  7.2 90.1 %all-gather.3.cloned.1.call-start = ((), (), s32[]{:S(2)}) async-start(), calls=%async_computation.3 | async-start | bytes 5406720 | tf_op jit(solution)/shard_map/all_gather | solution.py:21
  7.9 165.3 %reduce-scatter.6.cloned.1.call-start = ((), (), s32[]{:S(2)}) async-start(), calls=%async_computation.5 | async-start | bytes 7962624 | tf_op jit(solution)/shard_map/reduce_scatter | solution.py:32
  107.3 8.7 %copy-start.3 = (bf16[640,432]{0,1:T(8,128)(2,1)S(1)}, bf16[640,432]{0,1:T(8,128)(2,1)}, u32[]{:S(2)}) copy-start(bf16[640,432]{0,1:T(8,128)(2,1)} %param.10) | copy-start | bytes 1658884
  125.3 1.1 copy-start.6
  125.4 98.8 %reduce-scatter.4.cloned.1.call-start = ((), (), s32[]{:S(2)}) async-start(), calls=%async_computation.4 | async-start | bytes 7962624 | tf_op jit(solution)/shard_map/reduce_scatter | solution.py:31
  134.7 124.6 %all-gather.5.cloned.1.call-start = ((), (), s32[]{:S(2)}) async-start(), calls=%async_computation.6 | async-start | bytes 3981312 | tf_op jit(solution)/shard_map/all_gather | solution.py:35
  226.6 272.0 %reduce-scatter.8.cloned.1.call-start = ((), (), s32[]{:S(2)}) async-start(), calls=%async_computation.7 | async-start | bytes 10813440 | tf_op jit(solution)/shard_map/reduce_scatter | solution.py:36
  268.8 229.8 %copy-start.4 = (bf16[128,640]{1,0:T(8,128)(2,1)S(1)}, bf16[128,640]{1,0:T(8,128)(2,1)}, u32[]{:S(2)}) copy-start(bf16[128,640]{1,0:T(8,128)(2,1)} %param.8) | copy-start | bytes 491524
  268.8 310.5 %copy-start.1 = (bf16[640,256]{1,0:T(8,128)(2,1)S(1)}, bf16[640,256]{1,0:T(8,128)(2,1)}, u32[]{:S(2)}) copy-start(bf16[640,256]{1,0:T(8,128)(2,1)} %param.12) | copy-start | bytes 983044
  268.8 310.5 %copy-start.2 = (bf16[256,432]{0,1:T(8,128)(2,1)S(1)}, bf16[256,432]{0,1:T(8,128)(2,1)}, u32[]{:S(2)}) copy-start(bf16[256,432]{0,1:T(8,128)(2,1)} %param.13) | copy-start | bytes 663556
  579.1 2.0 copy-start.5
Sparse Core Ops, SparseCore 0:
  10.6 86.6 all-gather.2
  125.5 47.6 reduce-scatter.5
  175.8 48.3 reduce-scatter.3
  226.8 32.5 all-gather.4
  268.9 229.6 reduce-scatter.7
where the time goes:
time: 588 us
  waiting for transfers between devices  439 us (75%)
  blocking collectives  78.4 us (13%)
  matrix products  39 us (7%)
  between operations  13.8 us (2%)
  local copies, waits for them, and re-layouts  12.3 us (2%)
    reduce_scatter x1, waiting for transfers between devices, body(): lax.psum_scatter(jnp.dot(hidden_all, w_down, preferred_element_type=jnp.f...  230 us
    all_gather x1, waiting for transfers between devices, body(): every = lax.all_gather(tokens, 'row', axis=0, tiled=True)  86.9 us
    psum x1, blocking collectives, body(): fitness = lax.psum(placed, ('row', 'col'))  78.4 us
    reduce_scatter x1, waiting for transfers between devices, body(): lax.psum_scatter(gate_part, 'col', scatter_dimension=0, tiled=True)  51 us
    reduce_scatter x1, waiting for transfers between devices, body(): lax.psum_scatter(up_part, 'col', scatter_dimension=0, tiled=True)  38.4 us
    all_gather x1, waiting for transfers between devices, body(): hidden_all = lax.all_gather(hidden, 'col', axis=0, tiled=True)  32.6 us
  transfers between devices with their start and end apart: 5, of which 5 were waited for; matrix products, arithmetic and copies ran while one was open for 2% of the time, Pallas kernels for 0%

commit v1 on v0

--- a/solution.py
+++ b/solution.py
@@ -10,6 +10,13 @@
 sigma_scale = 0.5
 
 
+def gather_over(x, axis, d):
+    size = lax.axis_size(axis)
+    shards = jnp.stack([x for _ in range(size)])
+    shards = lax.all_to_all(shards, axis, split_axis=0, concat_axis=0)
+    return jnp.concatenate(shards, axis=d)
+
+
 def apply_factors(low_three, v_three):
     return jnp.einsum("psr,prf->psf", low_three, v_three, precision=lax.Precision.HIGHEST)
 
@@ -18,7 +25,7 @@
     dev_rows, dev_feat = tokens.shape
     members = factor_u.shape[1] // RANK
     units = w_up.shape[1]
-    every = lax.all_gather(tokens, "row", axis=0, tiled=True)
+    every = gather_over(tokens, "row", 0)
     total_rows = every.shape[0]
     gate_part = jnp.dot(every, w_gate, preferred_element_type=jnp.float32)
     up_part = jnp.dot(every, w_up, preferred_element_type=jnp.float32)

time: 588 us -> 634 us (1.078)
  waiting for transfers between devices: 439 us -> 470 us
  starting transfers between devices: 0.2 us -> 12.4 us
    all_to_all x0 -> x1, waiting for transfers between devices: none -> 114 us  [gather_over(): shards = lax.all_to_all(shards, axis, split_axis=0, concat_axis=0)]
    all_gather x1 -> x0, waiting for transfers between devices: 86.9 us -> none  [body(): every = lax.all_gather(tokens, 'row', axis=0, tiled=True)]
    all_to_all x0 -> x1, starting transfers between devices: none -> 12.3 us  [gather_over(): shards = lax.all_to_all(shards, axis, split_axis=0, concat_axis=0)]
  transfers between devices with their start and end apart: 5 -> 5, of which waited for: 5 -> 5; matrix products, arithmetic and copies ran while one was open for 2% -> 1% of each run, Pallas kernels for 0% -> 0%
where the time goes in v1:
time: 634 us; the launch traced here: 633 us
  waiting for transfers between devices  470 us (74%)
  blocking collectives  78.5 us (12%)
  matrix products  38.9 us (6%)
  local copies, waits for them, and re-layouts  14.4 us (2%)
  between operations  13.8 us (2%)
  starting transfers between devices  12.4 us (2%)
    reduce_scatter x1, waiting for transfers between devices, body(): lax.psum_scatter(jnp.dot(hidden_all, w_down, preferred_element_type=jnp.f...  230 us
    all_to_all x1, waiting for transfers between devices, gather_over(): shards = lax.all_to_all(shards, axis, split_axis=0, concat_axis=0)  114 us
    psum x1, blocking collectives, body(): fitness = lax.psum(placed, ('row', 'col'))  78.5 us
    reduce_scatter x1, waiting for transfers between devices, body(): lax.psum_scatter(gate_part, 'col', scatter_dimension=0, tiled=True)  50.9 us
    reduce_scatter x1, waiting for transfers between devices, body(): lax.psum_scatter(up_part, 'col', scatter_dimension=0, tiled=True)  43 us
    all_gather x1, waiting for transfers between devices, body(): hidden_all = lax.all_gather(hidden, 'col', axis=0, tiled=True)  32.6 us
  transfers between devices with their start and end apart: 5, of which 5 were waited for; matrix products, arithmetic and copies ran while one was open for 1% of the time, Pallas kernels for 0%

profile of v1, /device:TPU:1, one launch (start us, length us, event | category | flops | bytes accessed | tf_op | source)
XLA Modules:
  0.0 633.0 jit_solution(10957261019408826684)
XLA Ops:
  7.2 0.0 copy-start
  7.2 4.0 stack.2
  11.2 0.0 copy-start.1
  11.2 0.0 copy-start.2
  11.2 12.3 %all-to-all-start = ((bf16[32,128,640]{2,1,0:T(8,128)(2,1)}), bf16[32,128,640]{2,1,0:T(8,128)(2,1)}, u32[]{:S(2)}, u32[]{:S(2)}) async-start(bf16[32,128,640]{2,1,0:T(8,128)(2,1)} %stack.2), calls=%async_computation | async-start | bytes 10485760 | tf_op jit(solution)/shard_map/all_to_all | solution.py:16
  23.5 0.0 reduce-scatter.6.cloned.1.call-start
  23.5 0.0 copy-done.1
  23.5 0.2 copy.12
  23.7 0.1 reshape.24
  23.8 0.0 copy-done.2
  23.8 0.1 copy.13
  24.0 0.1 reshape.25
  24.0 113.9 %all-to-all-done = bf16[32,128,640]{2,1,0:T(8,128)(2,1)} async-done(((bf16[32,128,640]{2,1,0:T(8,128)(2,1)}), bf16[32,128,640]{2,1,0:T(8,128)(2,1)}, u32[]{:S(2)}, u32[]{:S(2)}) %all-to-all-start) | async-done | bytes 5242912 | tf_op jit(solution)/shard_map/all_to_all | solution.py:16
  138.0 4.2 fusion.4
  142.2 5.8 broadcast_multiply_fusion
  148.0 0.0 copy-start.3
  148.0 8.7 %copy.14 = f32[4096,432]{0,1:T(8,128)} copy(f32[4096,432]{1,0:T(8,128)} %bitcast.16) | data formatting | bytes 14155776 | tf_op jit(solution)/shard_map/mul | solution.py:36
  156.6 0.0 copy-done.3
  156.7 9.4 %convolution_add_fusion = f32[4096,432]{0,1:T(8,128)} fusion(f32[4096,432]{0,1:T(8,128)} %copy.14, bf16[4096,640]{1,0:T(8,128)(2,1)} %bitcast, bf16[640,432]{0,1:T(8,128)(2,1)S(1)} %copy-done.3), kind=kOutput, calls=%fused_computation | convolution fusion | flops 2266693632 | bytes 19951616 | tf_op jit(solution)/shard_map/dot_general | solution.py:31
  166.1 0.0 copy-start.6
  166.1 0.0 reduce-scatter.6.cloned.1.call-update
  166.1 0.0 reduce-scatter.4.cloned.1.call-start
  166.2 1.0 copy-done.6
  167.1 8.3 %fusion.3 = f32[4096,432]{0,1:T(8,128)} fusion(bf16[4096,640]{1,0:T(8,128)(2,1)} %bitcast, bf16[640,432]{0,1:T(8,128)(2,1)S(1)} %copy-done.6), kind=kOutput, calls=%fused_computation.9 | convolution fusion | flops 2264924160 | bytes 12873728 | tf_op jit(solution)/shard_map/dot_general | solution.py:30
  175.4 0.0 reduce-scatter.4.cloned.1.call-update
  175.5 0.0 all-gather.2.cloned.1.call-start
  175.5 43.0 %reduce-scatter.6.cloned.1.call-done = f32[512,432]{0,1:T(8,128)} async-done(((f32[4096,432]{0,1:T(8,128)}), f32[512,432]{0,1:T(8,128)}) %reduce-scatter.6.cloned.1.call-update) | async-done | bytes 884752 | tf_op jit(solution)/shard_map/reduce_scatter | solution.py:39
  218.6 50.9 %reduce-scatter.4.cloned.1.call-done = f32[512,432]{0,1:T(8,128)} async-done(((f32[4096,432]{0,1:T(8,128)}), f32[512,432]{0,1:T(8,128)}) %reduce-scatter.4.cloned.1.call-update) | async-done | bytes 884752 | tf_op jit(solution)/shard_map/reduce_scatter | solution.py:38
  269.5 2.5 multiply_convert_fusion
  272.0 0.0 all-gather.2.cloned.1.call-update
  272.0 0.0 reduce-scatter.8.cloned.1.call-start
  272.0 32.6 %all-gather.2.cloned.1.call-done = bf16[4096,432]{0,1:T(8,128)(2,1)} async-done(((bf16[512,432]{0,1:T(8,128)(2,1)}), bf16[4096,432]{0,1:T(8,128)(2,1)}) %all-gather.2.cloned.1.call-update) | async-done | bytes 3538960 | tf_op jit(solution)/shard_map/all_gather | solution.py:42
  304.7 0.0 copy-done
  304.7 9.4 %fusion.5 = f32[4096,640]{1,0:T(8,128)} fusion(bf16[4096,432]{0,1:T(8,128)(2,1)} %all-gather.2.cloned.1.call-done, bf16[432,640]{1,0:T(8,128)(2,1)S(1)} %copy-done), kind=kOutput, calls=%fused_computation.11 | convolution fusion | flops 2264924160 | bytes 14577664 | tf_op jit(solution)/shard_map/dot_general | solution.py:44
  314.1 0.0 copy-start.4
  314.1 0.0 reduce-scatter.8.cloned.1.call-update
  314.1 229.8 %reduce-scatter.8.cloned.1.call-done = f32[128,640]{1,0:T(8,128)} async-done(((f32[4096,640]{1,0:T(8,128)}), f32[128,640]{1,0:T(8,128)}) %reduce-scatter.8.cloned.1.call-update) | async-done | bytes 327696 | tf_op jit(solution)/shard_map/reduce_scatter | solution.py:43
  543.9 0.0 copy-done.4
  544.0 1.8 multiply_reduce_fusion
  545.7 0.1 reduce_sum.14
  545.8 0.1 reduce_sum.18
  545.9 0.1 multiply_dynamic-update-slice_fusion
  546.0 78.5 %psum.7 = f32[64]{0:T(128)S(1)} all-reduce(f32[64]{0:T(128)S(1)} %multiply_dynamic-update-slice_fusion), channel_id=1, replica_groups=mesh['row'=32,'col'=8] {'row','col'}, use_global_device_ids=true, to_apply=%region_5.6 | all-reduce | flops 64 | bytes 512 | tf_op jit(solution)/shard_map/psum | solution.py:56
  624.5 0.0 copy-start.5
  624.5 0.1 broadcast_in_dim.7
  624.6 0.1 mul.45
  624.7 1.8 convolution_multiply_fusion
  626.5 0.0 copy-done.5
  (1 shorter events, 0.0 us)
Async XLA Ops:
  7.2 297.5 %copy-start = (bf16[432,640]{1,0:T(8,128)(2,1)S(1)}, bf16[432,640]{1,0:T(8,128)(2,1)}, u32[]{:S(2)}) copy-start(bf16[432,640]{1,0:T(8,128)(2,1)} %param.11) | copy-start | bytes 1658884
  11.2 12.3 %copy-start.1 = (bf16[640,256]{1,0:T(8,128)(2,1)S(1)}, bf16[640,256]{1,0:T(8,128)(2,1)}, u32[]{:S(2)}) copy-start(bf16[640,256]{1,0:T(8,128)(2,1)} %param.12) | copy-start | bytes 983044
  11.2 12.6 %copy-start.2 = (bf16[256,432]{0,1:T(8,128)(2,1)S(1)}, bf16[256,432]{0,1:T(8,128)(2,1)}, u32[]{:S(2)}) copy-start(bf16[256,432]{0,1:T(8,128)(2,1)} %param.13) | copy-start | bytes 663556
  11.2 126.8 %all-to-all-start = ((bf16[32,128,640]{2,1,0:T(8,128)(2,1)}), bf16[32,128,640]{2,1,0:T(8,128)(2,1)}, u32[]{:S(2)}, u32[]{:S(2)}) async-start(bf16[32,128,640]{2,1,0:T(8,128)(2,1)} %stack.2), calls=%async_computation | async-start | bytes 10485760 | tf_op jit(solution)/shard_map/all_to_all | solution.py:16
  23.5 195.1 %reduce-scatter.6.cloned.1.call-start = ((), (), s32[]{:S(2)}) async-start(), calls=%async_computation.5 | async-start | bytes 7962624 | tf_op jit(solution)/shard_map/reduce_scatter | solution.py:39
  148.0 8.7 %copy-start.3 = (bf16[640,432]{0,1:T(8,128)(2,1)S(1)}, bf16[640,432]{0,1:T(8,128)(2,1)}, u32[]{:S(2)}) copy-start(bf16[640,432]{0,1:T(8,128)(2,1)} %param.10) | copy-start | bytes 1658884
  166.1 1.1 copy-start.6
  166.1 103.4 %reduce-scatter.4.cloned.1.call-start = ((), (), s32[]{:S(2)}) async-start(), calls=%async_computation.4 | async-start | bytes 7962624 | tf_op jit(solution)/shard_map/reduce_scatter | solution.py:38
  175.5 129.2 %all-gather.2.cloned.1.call-start = ((), (), s32[]{:S(2)}) async-start(), calls=%async_computation.6 | async-start | bytes 3981312 | tf_op jit(solution)/shard_map/all_gather | solution.py:42
  272.0 272.0 %reduce-scatter.8.cloned.1.call-start = ((), (), s32[]{:S(2)}) async-start(), calls=%async_computation.7 | async-start | bytes 10813440 | tf_op jit(solution)/shard_map/reduce_scatter | solution.py:43
  314.1 229.8 %copy-start.4 = (bf16[128,640]{1,0:T(8,128)(2,1)S(1)}, bf16[128,640]{1,0:T(8,128)(2,1)}, u32[]{:S(2)}) copy-start(bf16[128,640]{1,0:T(8,128)(2,1)} %param.8) | copy-start | bytes 491524
  624.5 2.0 copy-start.5
Sparse Core Ops, SparseCore 0:
  166.2 52.2 reduce-scatter.5
  221.1 48.3 reduce-scatter.3
  272.1 32.5 all-gather.1
  314.3 229.6 reduce-scatter.7
